TPU v7x, 1024 devices: a whole 8x8x8 slice. The times are simulated.
1024 devices in a mesh: node: 64 (over z, y), local: 16 (over x, core).
Axes of the slice: x: 8, y: 8, z: 8, core: 2. Of those that a mesh axis runs over, the one named last changes fastest.
Arguments:
- tokens: bfloat16 [6144, 7168], P('node', 'local'), may hold values from -6 to 6
- expert_ids: int32 [6144, 8], P('node'), may hold values from 0 to 15, all different within a row; in each aligned block of 96 rows (0 to 95, 96 to 191, ...) at most 72 rows name the same one
- route_weight: float32 [6144, 8], P('node'), may hold values from 0.05 to 0.4
- pool_offset: int32 [64, 16], P('node'), may hold values from 0 to 3
- gate_up: bfloat16 [64, 7168, 2048], P('node', 'local'), may hold values from -0.0625 to 0.0625
- down_proj: bfloat16 [64, 1024, 7168], P('node', None, 'local'), may hold values from -0.1875 to 0.1875
- shared_gate_up: bfloat16 [7168, 2048], P('local'), may hold values from -0.0625 to 0.0625
- shared_down: bfloat16 [1024, 7168], P(None, 'local'), may hold values from -0.1875 to 0.1875
Outputs:
- mixed: bfloat16 [6144, 7168], P('node', 'local')
Inputs may be any that keep to these rules, and one draw needn't show every extreme that they name: `expert_ids`: each row names 8 different experts; within the 96 rows of one node no expert is named more than 72 times, and in some node one expert is named exactly 72 times.
All inputs are finite; a program needn't handle non-finite values.
Results may differ from a plain program's by a relative error of at most 0.03.
Values may be sent and summed in bfloat16 or wider, within the bound.
A program may use at most 64 MiB of HBM per device.

v0:
```python
import jax
import jax.numpy as jnp
from jax import lax
from jax.sharding import PartitionSpec as P


def expert_terms(weights, rows):
    return lax.dot_general(
        weights, rows, (((0,), (1,)), ((), ())), preferred_element_type=jnp.float32
    )


def activate(gate, upper):
    return (jax.nn.silu(gate) * upper).astype(jnp.bfloat16)


def grouped_activate(partial_value, groups):
    blocks = partial_value.reshape(groups, 2, -1, partial_value.shape[1])
    return activate(blocks[:, 0], blocks[:, 1]).reshape(-1, partial_value.shape[1])


def shards(
    tokens, expert_ids, route_weight, pool_offset, gate_up, down_proj, shared_gate_up, shared_down
):
    tok_count, top_count = expert_ids.shape
    experts = pool_offset.shape[1]
    node_count = lax.axis_size("node")
    groups = lax.axis_size("local")
    pools = node_count // experts
    bound_most = 3 * tok_count * top_count // (2 * experts)
    capacity = bound_most // pools
    slot_count = node_count * capacity
    width_local = tokens.shape[1]
    matches = (expert_ids[:, :, None] == jnp.arange(experts, dtype=jnp.int32)).astype(jnp.int32)
    per_token = matches.sum(axis=1)
    before = jnp.cumsum(per_token, axis=0) - per_token
    arrival_rank = jnp.sum(matches * before[:, None, :], axis=2)
    offset = jnp.sum(matches * pool_offset[0][None, None, :], axis=2)
    target = (arrival_rank + offset) % pools * experts + expert_ids
    position = target * capacity + arrival_rank // pools
    placed = position[:, :, None] == jnp.arange(slot_count, dtype=jnp.int32)
    routing = placed.sum(axis=1).astype(jnp.bfloat16)
    outgoing = lax.dot_general(
        routing, tokens, (((0,), (0,)), ((), ())), preferred_element_type=jnp.float32
    ).astype(jnp.bfloat16)
    outgoing = outgoing.reshape(node_count, capacity, width_local)
    arrived = lax.all_to_all(outgoing, "node", split_axis=0, concat_axis=0, tiled=True)
    arrived_rows = arrived.reshape(slot_count, width_local)
    expert_term = expert_terms(gate_up[0], arrived_rows)
    shared_term = expert_terms(shared_gate_up, tokens)
    partial_value, shared_partial = (
        lax.psum_scatter(
            expert_term.astype(jnp.bfloat16), "local", scatter_dimension=1, tiled=True
        ).astype(jnp.float32),
        lax.psum_scatter(
            shared_term.astype(jnp.bfloat16), "local", scatter_dimension=1, tiled=True
        ).astype(jnp.float32),
    )
    hidden = grouped_activate(partial_value, groups)
    shared_hidden = grouped_activate(shared_partial, groups)
    hidden, shared_hidden = (
        lax.all_gather(hidden, "local", axis=1, tiled=True),
        lax.all_gather(shared_hidden, "local", axis=1, tiled=True),
    )
    expert_out = lax.dot_general(
        hidden, down_proj[0], (((0,), (0,)), ((), ())), preferred_element_type=jnp.float32
    ).astype(jnp.bfloat16)
    returned = lax.all_to_all(
        expert_out.reshape(node_count, capacity, width_local),
        "node",
        split_axis=0,
        concat_axis=0,
        tiled=True,
    )
    returned = returned.reshape(slot_count, width_local)
    combiner = jnp.sum(placed.astype(jnp.float32) * route_weight[:, :, None], axis=1)
    routed = jnp.dot(combiner, returned.astype(jnp.float32), precision=lax.Precision.HIGHEST)
    shared_out = lax.dot_general(
        shared_hidden, shared_down, (((0,), (0,)), ((), ())), preferred_element_type=jnp.float32
    )
    return (shared_out + routed).astype(jnp.bfloat16)


def solution(mesh):
    placed = (
        P("node", "local"),
        P("node", None),
        P("node", None),
        P("node", None),
        P("node", "local", None),
        P("node", None, "local"),
        P("local", None),
        P(None, "local"),
    )
    return jax.shard_map(
        shards, mesh=mesh, in_specs=placed, out_specs=P("node", "local"), check_vma=False
    )
```

profile of v0, /device:TPU:1, one launch (start us, length us, event | category | flops | bytes accessed | tf_op | source)
XLA Modules:
  0.0 322.8 jit_solution(687545328716378285)
XLA Ops:
  9.3 1.1 convert_reduce_fusion
  10.4 1.4 convolution_convert_fusion.1
  11.8 1.7 copy.27
  13.4 2.4 reshape.45
  15.8 62.8 %all_to_all.10 = bf16[64,18,448]{2,1,0:T(8,128)(2,1)} all-to-all(bf16[64,18,448]{2,1,0:T(8,128)(2,1)S(1)} %reshape.45), channel_id=1, replica_groups=mesh['node'=64,'local'=16] {'node'}, dimensions={0} | all-to-all | bytes 2064384 | tf_op jit(solution)/shard_map/all_to_all | solution.py:47
  78.6 2.4 reshape.46
  81.1 4.3 %fusion.1 = bf16[2048,1152]{0,1:T(8,128)(2,1)} fusion(bf16[1152,448]{1,0:T(8,128)(2,1)S(1)} %reshape.46, bf16[1,448,2048]{2,1,0:T(8,128)(2,1)S(1)} %copy-done), kind=kOutput, calls=%fused_computation.1 | convolution fusion | flops 2116288512 | bytes 7585792 | tf_op jit(solution)/shard_map/dot_general | solution.py:8
  85.4 66.4 %reduce-scatter.4.cloned.1.call-done = bf16[2048,72]{0,1:T(8,128)(2,1)} async-done(((bf16[2048,1152]{0,1:T(8,128)(2,1)}), bf16[2048,72]{0,1:T(8,128)(2,1)}) %reduce-scatter.4.cloned.1.call-update) | async-done | bytes 294928 | tf_op jit(solution)/shard_map/reduce_scatter | solution.py:52
  151.8 1.8 reshape.54
  153.7 4.2 %slice_reduce_fusion.1 = (f32[16,64,72]{1,0,2:T(8,128)}, f32[16,64,72]{1,0,2:T(8,128)}) fusion(f32[16,2,64,72]{2,1,0,3:T(2,128)S(1)} %reshape.54), kind=kLoop, calls=%fused_computation.13 | loop fusion | bytes 1179648 | tf_op jit(solution)/shard_map/slice | solution.py:19
  157.9 1.3 squeeze.21
  159.2 1.2 squeeze.22
  161.2 45.7 %all-gather.3.cloned.1.call-done = bf16[1024,1152]{0,1:T(8,128)(2,1)} async-done(((bf16[1024,72]{0,1:T(8,128)(2,1)}), bf16[1024,1152]{0,1:T(8,128)(2,1)}) %all-gather.3.cloned.1.call-update) | async-done | bytes 2359312 | tf_op jit(solution)/shard_map/all_gather | solution.py:62
  206.9 4.0 %convolution_convert_fusion.2 = bf16[1152,448]{0,1:T(8,128)(2,1)} fusion(bf16[1024,1152]{0,1:T(8,128)(2,1)} %all-gather.3.cloned.1.call-done, bf16[1,1024,448]{1,2,0:T(8,128)(2,1)S(1)} %copy-done.2), kind=kOutput, calls=%fused_computation.6 | convolution fusion | flops 1057480704 | bytes 4308992 | tf_op jit(solution)/shard_map/dot_general | solution.py:65
  210.9 1.7 copy.28
  212.7 1.4 reshape.49
  214.0 14.1 %all-to-all-start.1 = ((bf16[64,18,448]{2,1,0:T(8,128)(2,1)}), bf16[64,18,448]{2,1,0:T(8,128)(2,1)S(1)}, u32[]{:S(2)}, u32[]{:S(2)}) async-start(bf16[64,18,448]{2,1,0:T(8,128)(2,1)} %reshape.49), calls=%async_computation.2 | async-start | bytes 3145728 | tf_op jit(solution)/shard_map/all_to_all | solution.py:68
  228.2 2.7 convolution_convert_fusion.3
  230.9 28.7 %fusion = bf16[2048,8]{0,1:T(8,128)(2,1)S(1)} fusion(bf16[2048,96]{0,1:T(8,128)(2,1)} %convolution_convert_fusion.3), kind=kCustom, calls=%all-reduce-scatter | all-reduce-scatter fusion | flops 262145 | bytes 430080
  259.6 1.9 collective-permute-start
  261.5 1.9 collective-permute-start.1
  263.5 5.5 %collective-permute-start.2 = (bf16[2048,8]{0,1:T(8,128)(2,1)S(1)}, bf16[2048,8]{0,1:T(8,128)(2,1)}, u32[]{:S(2)}, u32[]{:S(2)}) collective-permute-start(bf16[2048,8]{0,1:T(8,128)(2,1)S(1)} %fusion), channel_id=1, source_target_pairs={{0,3},{1,4},{2,5},{3,6},{4,7},{5,8},{6,9},{7,10},{8,11},{9,12},{10... | collective-permute-start | bytes 98312
  269.6 4.7 %collective-permute-start.3 = (bf16[2048,6]{0,1:T(8,128)(2,1)}, bf16[2048,6]{0,1:T(8,128)(2,1)}, u32[]{:S(2)}, u32[]{:S(2)}) collective-permute-start(bf16[2048,6]{0,1:T(8,128)(2,1)} %slice.20), channel_id=1, source_target_pairs={{0,4},{1,5},{2,6},{3,7},{4,8},{5,9},{6,10},{7,11},{8,12},{9,13},{1... | collective-permute-start | bytes 73736
  275.1 1.9 select_reduce_fusion
  277.0 1.3 dynamic-slice.4
  279.0 7.4 %concatenate = bf16[2048,38]{0,1:T(8,128)(2,1)} concatenate(bf16[2048,6]{0,1:T(8,128)(2,1)} %collective-permute-done.3, bf16[2048,8]{0,1:T(8,128)(2,1)} %collective-permute-done.2, bf16[2048,8]{0,1:T(8,128)(2,1)} %collective-permute-done.1, bf16[2048,8]{0,1:T(8,128)(2,1)} %collective-permute-done, bf16[2048,8]{0,1:T(8,128)(2,1)S(1)} %fusion), dimensions={1} | concatenate | bytes 311296
  286.4 1.5 dynamic-slice_convert_fusion
  290.6 17.0 %all-gather = bf16[16,6,1024]{2,1,0:T(8,128)(2,1)} all-gather(bf16[1,6,1024]{2,1,0:T(8,128)(2,1)S(1)} %fusion.6), channel_id=1, replica_groups=mesh['node'=64,'local'=16] {'local'}, dimensions={0}, use_global_device_ids=true | all-gather | bytes 208896 | tf_op jit(solution)/shard_map/all_gather | solution.py:63
  307.7 1.7 reshape.56
  309.4 2.4 fusion.14
  311.8 1.4 reshape.50
  313.2 2.8 fusion.3
  (31 shorter events, 7.7 us)
Async XLA Ops:
  6.5 74.5 %copy-start = (bf16[1,448,2048]{2,1,0:T(8,128)(2,1)S(1)}, bf16[1,448,2048]{2,1,0:T(8,128)(2,1)}, u32[]{:S(2)}) copy-start(bf16[1,448,2048]{2,1,0:T(8,128)(2,1)} %param.12) | copy-start | bytes 5505028
  6.5 145.3 %reduce-scatter.4.cloned.1.call-start = ((), (), s32[]{:S(2)}) async-start(), calls=%async_computation.3 | async-start | bytes 5013504 | tf_op jit(solution)/shard_map/reduce_scatter | solution.py:52
  85.4 121.5 %all-gather.3.cloned.1.call-start = ((), (), s32[]{:S(2)}) async-start(), calls=%async_computation.4 | async-start | bytes 2506752 | tf_op jit(solution)/shard_map/all_gather | solution.py:62
  157.9 49.0 %copy-start.2 = (bf16[1,1024,448]{1,2,0:T(8,128)(2,1)S(1)}, bf16[1,1024,448]{1,2,0:T(8,128)(2,1)}, u32[]{:S(2)}) copy-start(bf16[1,1024,448]{1,2,0:T(8,128)(2,1)} %param.13) | copy-start | bytes 2752516
  214.0 14.2 %copy-start.1 = (bf16[96,448]{1,0:T(8,128)(2,1)S(1)}, bf16[96,448]{1,0:T(8,128)(2,1)}, u32[]{:S(2)}) copy-start(bf16[96,448]{1,0:T(8,128)(2,1)} %param.8) | copy-start | bytes 258052
  214.0 97.7 %all-to-all-start.1 = ((bf16[64,18,448]{2,1,0:T(8,128)(2,1)}), bf16[64,18,448]{2,1,0:T(8,128)(2,1)S(1)}, u32[]{:S(2)}, u32[]{:S(2)}) async-start(bf16[64,18,448]{2,1,0:T(8,128)(2,1)} %reshape.49), calls=%async_computation.2 | async-start | bytes 3145728 | tf_op jit(solution)/shard_map/all_to_all | solution.py:68
  259.6 19.4 %collective-permute-start = (bf16[2048,8]{0,1:T(8,128)(2,1)S(1)}, bf16[2048,8]{0,1:T(8,128)(2,1)}, u32[]{:S(2)}, u32[]{:S(2)}) collective-permute-start(bf16[2048,8]{0,1:T(8,128)(2,1)S(1)} %fusion), channel_id=1, source_target_pairs={{0,1},{1,2},{2,3},{3,4},{4,5},{5,6},{6,7},{7,8},{8,9},{9,10},{10,1... | collective-permute-start | bytes 98312
  261.5 17.5 %collective-permute-start.1 = (bf16[2048,8]{0,1:T(8,128)(2,1)S(1)}, bf16[2048,8]{0,1:T(8,128)(2,1)}, u32[]{:S(2)}, u32[]{:S(2)}) collective-permute-start(bf16[2048,8]{0,1:T(8,128)(2,1)S(1)} %fusion), channel_id=1, source_target_pairs={{0,2},{1,3},{2,4},{3,5},{4,6},{5,7},{6,8},{7,9},{8,10},{9,11},{10,... | collective-permute-start | bytes 98312
  263.5 15.6 %collective-permute-start.2 = (bf16[2048,8]{0,1:T(8,128)(2,1)S(1)}, bf16[2048,8]{0,1:T(8,128)(2,1)}, u32[]{:S(2)}, u32[]{:S(2)}) collective-permute-start(bf16[2048,8]{0,1:T(8,128)(2,1)S(1)} %fusion), channel_id=1, source_target_pairs={{0,3},{1,4},{2,5},{3,6},{4,7},{5,8},{6,9},{7,10},{8,11},{9,12},{10... | collective-permute-start | bytes 98312
  269.6 9.4 %collective-permute-start.3 = (bf16[2048,6]{0,1:T(8,128)(2,1)}, bf16[2048,6]{0,1:T(8,128)(2,1)}, u32[]{:S(2)}, u32[]{:S(2)}) collective-permute-start(bf16[2048,6]{0,1:T(8,128)(2,1)} %slice.20), channel_id=1, source_target_pairs={{0,4},{1,5},{2,6},{3,7},{4,8},{5,9},{6,10},{7,11},{8,12},{9,13},{1... | collective-permute-start | bytes 73736
Sparse Core Ops, SparseCore 0:
  85.5 66.2 reduce-scatter.3
  161.3 45.5 all-gather.2
where the time goes:
time: 324 us; the launch traced here: 323 us
  waiting for transfers between devices  112 us (35%)
  blocking collectives  109 us (34%)
  local copies, waits for them, and re-layouts  34.4 us (11%)
  starting transfers between devices  28.3 us (9%)
  matrix products  17.5 us (5%)
  between operations  14.2 us (4%)
  other arithmetic  7.74 us (2%)
    reduce_scatter x1, waiting for transfers between devices, shards(): lax.psum_scatter(expert_term.astype(jnp.bfloat16), 'local', scatter_dimen...  66.4 us
    all_to_all x1, blocking collectives, shards(): lax.all_to_all(outgoing, 'node', split_axis=0, concat_axis=0, tiled=True)  62.8 us
    all_gather x1, waiting for transfers between devices, shards(): lax.all_gather(hidden, 'local', axis=1, tiled=True)  45.7 us
    unnamed x1, blocking collectives  28.7 us
    all_gather x1, blocking collectives, shards(): lax.all_gather(shared_hidden, 'local', axis=1, tiled=True)  17 us
    all_to_all x1, starting transfers between devices, shards(): lax.all_to_all(expert_out.reshape(node_count, capacity, width_local), 'no...  14.1 us
    unnamed x4, starting transfers between devices  14.1 us
    unnamed x11, local copies, waits for them, and re-layouts  11.8 us
  transfers between devices with their start and end apart: 7, of which 2 were waited for; matrix products, arithmetic and copies ran while one was open for 16% of the time, Pallas kernels for 0%

commit v1 on v0

v1 whole, which is shorter than its diff:
```python
import functools
import math

import jax
import jax.numpy as jnp
from jax import lax
from jax.experimental import pallas as pl
from jax.experimental.pallas import tpu as pltpu
from jax.sharding import PartitionSpec as P

MESH = pl.DeviceIdType.MESH
MOST = 72
BLOCKS_PER_CHUNK = 2
TICKS_APART = 3
F32 = jnp.float32
BF16 = jnp.bfloat16


def dot(a, b):
    return jnp.dot(a, b, preferred_element_type=F32)


def kernel(
    cfg,
    ids_ref, wt_ref, off_ref, tok_ref, gu_hbm, dn_hbm, sgu_hbm, sdn_hbm,
    out_ref,
    gu, sgu, dn, sdn, tok2, toks, meta, codes, weights, xs, xsend, ps, pbuf, rmaj, rmin, hid, hs, obuf, rbuf, comb,
    part, prec, acc, fsend, frecv,
    part_s, part_r, loc_sem, tok_s, tok_r, meta_s, meta_r, disp_s, disp_r,
    maj_s, maj_r, min_s, min_r, gmaj_s, gmaj_r, gmin_s, gmin_r, ret_s, ret_r, sum_s, sum_r,
):
    side, nx, experts, pools, half, rows = (cfg[k] for k in ("side", "nx", "experts", "pools", "half", "rows"))
    per, apart = cfg["per"], cfg["apart"]
    tn = tok_ref.shape[0]
    width = tok_ref.shape[1]
    th = tn // 2
    chunks = side // per
    unit_cols = pbuf.shape[3]
    kept = half * side
    shift_pool, shift_side = pools.bit_length() - 1, side.bit_length() - 1

    n, l = lax.axis_index("node"), lax.axis_index("local")
    x, c = lax.div(l, 2), lax.rem(l, 2)
    z, y = lax.div(n, side), lax.rem(n, side)
    a1 = y * (1 - c) + z * c
    a2 = z * (1 - c) + y * c
    stride1 = 1 + (side - 1) * c
    stride2 = side - (side - 1) * c
    sgn = 1 - 2 * c

    def ring(i, count):
        return lax.rem(i + 2 * count, count)

    def node_at(i1, i2):
        return i1 * stride1 + i2 * stride2

    partner = (n, x * 2 + 1 - c)

    def x_peer(step):
        return (n, ring(x + step, nx) * 2 + c)

    def first_peer(step):
        return (node_at(ring(a1 + step, side), a2), l)

    def second_peer(step):
        return (node_at(a1, ring(a2 + step, side)), l)

    offsets = [0]
    for d in range(1, side // 2 + 1):
        offsets += [d, -d]
    offsets = offsets[:side]
    pending = []

    def send(src, dst, s, r, to):
        copy = pltpu.make_async_remote_copy(
            src_ref=src, dst_ref=dst, send_sem=s, recv_sem=r, device_id=to, device_id_type=MESH
        )
        copy.start()
        pending.append(copy)

    def arrived(dst, s, r):
        pltpu.make_async_remote_copy(
            src_ref=dst, dst_ref=dst, send_sem=s, recv_sem=r, device_id=partner, device_id_type=MESH
        ).wait_recv()

    barrier = pltpu.get_barrier_semaphore()
    greeted = [partner, x_peer(1), x_peer(-1)]
    greeted += [first_peer(d) for d in range(1, side)] + [second_peer(d) for d in range(1, side)]
    for to in greeted:
        pl.semaphore_signal(barrier, inc=1, device_id=to, device_id_type=MESH)

    gu_rows = pl.ds(pl.multiple_of(c * width, 16), width)
    own = [
        pltpu.make_async_copy(sgu_hbm, sgu.at[gu_rows], loc_sem.at[0]),
        pltpu.make_async_copy(gu_hbm, gu.at[gu_rows], loc_sem.at[1]),
        pltpu.make_async_copy(dn_hbm, dn.at[c], loc_sem.at[2]),
        pltpu.make_async_copy(sdn_hbm, sdn.at[c], loc_sem.at[3]),
    ]
    for copy in own:
        copy.start()

    ids, wt = ids_ref[...], wt_ref[...]
    expert = lax.broadcasted_iota(jnp.int32, (experts, tn), 0)
    named = jnp.zeros((experts, tn), F32)
    gate_weight = jnp.zeros((experts, tn), F32)
    for k in range(ids.shape[0]):
        hit = ids[k : k + 1, :] == expert
        named = named + jnp.where(hit, 1.0, 0.0)
        gate_weight = gate_weight + jnp.where(hit, wt[k : k + 1, :], 0.0)
    earlier = jnp.where(
        lax.broadcasted_iota(jnp.int32, (tn, tn), 0) < lax.broadcasted_iota(jnp.int32, (tn, tn), 1), 1.0, 0.0
    ).astype(BF16)
    rank = dot(named.astype(BF16), earlier).astype(jnp.int32)
    code = ((rank + off_ref[...]) & (pools - 1)) * 32 + (rank >> shift_pool)
    code = jnp.where(named > 0.0, code.astype(F32), -1.0)
    meta[a1] = jnp.concatenate([code, gate_weight], axis=0)
    tok2[c] = tok_ref[...]

    pl.semaphore_wait(barrier, len(greeted))

    send(tok_ref, tok2.at[c], part_s.at[0], part_r.at[0], partner)
    for d in range(1, side):
        send(meta.at[a1], meta.at[a1], meta_s.at[d - 1], meta_r.at[d - 1], first_peer(d))
    send(sgu_hbm, sgu.at[gu_rows], part_s.at[1], part_r.at[1], partner)
    send(gu_hbm, gu.at[gu_rows], part_s.at[2], part_r.at[2], partner)
    send(dn_hbm, dn.at[c], part_s.at[3], part_r.at[3], partner)
    send(sdn_hbm, sdn.at[c], part_s.at[4], part_r.at[4], partner)

    other_rows = pl.ds(pl.multiple_of((1 - c) * width, 16), width)
    arrived(tok2.at[1 - c], part_s.at[0], part_r.at[0])
    toks[a1] = jnp.concatenate([tok2[0], tok2[1]], axis=1)

    long_way, short_way = side // 2, side - 1 - side // 2

    def token_hop(h, direction, piece):
        hops = long_way if (direction > 0) == (piece == 0) else short_way
        if h > hops:
            return
        index = ring(a1 - direction * (h - 1), side)
        slot = (h - 1) * 4 + piece * 2 + (direction > 0)
        view = toks.at[index, pl.ds(piece * th, th)]
        send(view, view, tok_s.at[slot], tok_r.at[slot], first_peer(direction))

    def token_wait(h, direction, piece):
        hops = long_way if (direction > 0) == (piece == 0) else short_way
        if h > hops:
            return
        index = ring(a1 - direction * h, side)
        slot = (h - 1) * 4 + piece * 2 + (direction > 0)
        arrived(toks.at[index, pl.ds(piece * th, th)], tok_s.at[slot], tok_r.at[slot])

    ways = [(1, 0), (-1, 1), (1, 1), (-1, 0)]
    for h in range(1, long_way + 1):
        for direction, piece in ways:
            if h > 1:
                token_wait(h - 1, direction, piece)
            token_hop(h, direction, piece)

    own[0].wait()
    arrived(sgu.at[other_rows], part_s.at[1], part_r.at[1])
    mine = toks[a1, pl.ds(pl.multiple_of(c * th, 16), th), :]
    ps[...] = jnp.zeros_like(ps)

    def shared_step(q, carry):
        cols = pl.ds(pl.multiple_of(q * unit_cols, 128), unit_cols)
        ps[q, 0:th, :] = dot(mine, sgu[:, cols])
        return carry

    lax.fori_loop(0, nx, shared_step, 0)

    for d in range(1, side):
        arrived(meta.at[ring(a1 - d, side)], meta_s.at[d - 1], meta_r.at[d - 1])
    codes[...] = jnp.concatenate([meta[i, 0:experts, :] + 128.0 * i for i in range(side)], axis=1)
    weights[...] = jnp.concatenate([meta[i, experts:, :] for i in range(side)], axis=1)

    for direction, piece in ways:
        token_wait(long_way, direction, piece)

    row = lax.broadcasted_iota(jnp.int32, (rows, 1), 0)

    def matches(b):
        m = node_at(a1, ring(a2 + offsets[b], side))
        p, e = lax.div(m, experts), lax.rem(m, experts)
        want = (row & (side - 1)) * 128 + (row >> shift_side) + (p * 32 + half * c)
        want = jnp.where(row < kept, want, -5).astype(F32)
        return codes[pl.ds(e, 1), :] == want, weights[pl.ds(e, 1), :]

    flat_toks = toks[...].reshape(side * tn, 2 * width)
    for k in range(chunks):
        chosen = jnp.concatenate(
            [jnp.where(matches(k * per + i)[0], 1.0, 0.0) for i in range(per)], axis=0
        ).astype(BF16)
        picked = dot(chosen, flat_toks).astype(BF16)
        for i in range(per):
            b = k * per + i
            block = picked[i * rows : (i + 1) * rows]
            if b == 0:
                xs[0] = block
            else:
                xsend[b] = block
                send(xsend.at[b], xs.at[b], disp_s.at[b - 1], disp_r.at[b - 1], second_peer(offsets[b]))

    own[1].wait()
    arrived(gu.at[other_rows], part_s.at[2], part_r.at[2])

    hmaj, hmin = nx // 2, nx - 1 - nx // 2

    def to_x(off):
        return ring(x + sgn * off, nx)

    def start_chunk(k):
        for i in range(per):
            b = k * per + i
            if b > 0:
                arrived(xs.at[b], disp_s.at[b - 1], disp_r.at[b - 1])
        rows_in = xs[k * per : (k + 1) * per].reshape(per * rows, 2 * width)

        def step(i, carry):
            q = to_x(hmaj - i)
            cols = pl.ds(pl.multiple_of(q * unit_cols, 128), unit_cols)
            value = dot(rows_in, gu[:, cols])
            shared = ps[q, k * per * 8 : (k + 1) * per * 8, :]
            pieces = []
            for j in range(per):
                pieces += [value[j * rows : j * rows + kept], shared[j * 8 : (j + 1) * 8]]
            pbuf[k, q] = jnp.concatenate(pieces, axis=0).astype(BF16)
            return carry

        lax.fori_loop(0, nx, step, 0)
        send(pbuf.at[k, to_x(hmaj)], rmaj.at[k, 0], maj_s.at[k * hmaj], maj_r.at[k * hmaj], x_peer(sgn))
        if hmin:
            send(pbuf.at[k, to_x(-hmin)], rmin.at[k, 0], min_s.at[k * hmin], min_r.at[k * hmin], x_peer(-sgn))

    def sum_hop(k, h, hops, way, recv, s, r):
        slot = k * hops + h
        arrived(recv.at[k, h - 1], s.at[slot - 1], r.at[slot - 1])
        q = to_x(way * (hops - h))
        pbuf[k, q] = (pbuf[k, q].astype(F32) + recv[k, h - 1].astype(F32)).astype(BF16)
        send(pbuf.at[k, q], recv.at[k, h], s.at[slot], r.at[slot], x_peer(sgn * way))

    def activate(k):
        slot = k * hmaj + hmaj - 1
        arrived(rmaj.at[k, hmaj - 1], maj_s.at[slot], maj_r.at[slot])
        total = pbuf[k, x].astype(F32) + rmaj[k, hmaj - 1].astype(F32)
        if hmin:
            slot = k * hmin + hmin - 1
            arrived(rmin.at[k, hmin - 1], min_s.at[slot], min_r.at[slot])
            total = total + rmin[k, hmin - 1].astype(F32)
        wide = unit_cols // 2
        left, right = total[:, :wide], total[:, wide:]
        low = lax.broadcasted_iota(jnp.int32, left.shape, 1) < wide // 2
        gate = jnp.where(low, left, pltpu.roll(right, wide // 2, 1))
        upper = jnp.where(low, pltpu.roll(left, wide // 2, 1), right)
        hid[k, x] = (gate / (1.0 + jnp.exp(-gate)) * upper).astype(BF16)
        gather_hop(k, 1, hmaj, 1, gmaj_s, gmaj_r)
        gather_hop(k, 1, hmin, -1, gmin_s, gmin_r)

    def gather_hop(k, h, hops, way, s, r):
        if h > hops:
            return
        view = hid.at[k, to_x(-way * (h - 1))]
        slot = k * hops + h - 1
        send(view, view, s.at[slot], r.at[slot], x_peer(sgn * way))

    def gather_wait(k, h, hops, way, s, r):
        if h > hops:
            return
        slot = k * hops + h - 1
        arrived(hid.at[k, to_x(-way * h)], s.at[slot], r.at[slot])

    def finish_chunk(k):
        if k == 0:
            own[2].wait()
            arrived(dn.at[1 - c], part_s.at[3], part_r.at[3])
        hidden = jnp.concatenate([hid[k, q] for q in range(nx)], axis=1)
        both = [dot(hidden, dn[i]) for i in range(2)]
        result = jnp.concatenate(both, axis=1).astype(BF16)
        for i in range(per):
            b = k * per + i
            block = result[i * rows : (i + 1) * rows]
            if b == 0:
                rbuf[0] = block
            else:
                obuf[b] = block
                send(obuf.at[b], rbuf.at[b], ret_s.at[b - 1], ret_r.at[b - 1], second_peer(-offsets[b]))
        for i in range(per):
            b = k * per + i
            if b * 8 < th:
                top = (i + 1) * rows - 16
                hs[b * 8 : (b + 1) * 8, :] = hidden[top : top + 16].astype(F32)[8:16]

    def stage(k, s):
        if s == 0:
            start_chunk(k)
        elif s < hmaj:
            sum_hop(k, s, hmaj, 1, rmaj, maj_s, maj_r)
            if s < hmin:
                sum_hop(k, s, hmin, -1, rmin, min_s, min_r)
        elif s == hmaj:
            activate(k)
        else:
            h = s - hmaj
            gather_wait(k, h, hmaj, 1, gmaj_s, gmaj_r)
            gather_hop(k, h + 1, hmaj, 1, gmaj_s, gmaj_r)
            gather_wait(k, h, hmin, -1, gmin_s, gmin_r)
            gather_hop(k, h + 1, hmin, -1, gmin_s, gmin_r)
            if h == hmaj:
                finish_chunk(k)

    stages = 2 * hmaj + 1
    for tick in range((chunks - 1) * apart + stages):
        for k in range(chunks):
            s = tick - k * apart
            if 0 <= s < stages:
                stage(k, s)

    own[3].wait()
    arrived(sdn.at[1 - c], part_s.at[4], part_r.at[4])
    shared_hidden = hs[...].astype(BF16)
    shared_out = jnp.concatenate([dot(shared_hidden, sdn[i]) for i in range(2)], axis=1)

    for b in range(side):
        hit, weight = matches(b)
        comb[b * rows : (b + 1) * rows, :] = jnp.where(hit, weight, 0.0).astype(BF16)
    for b in range(1, side):
        arrived(rbuf.at[b], ret_s.at[b - 1], ret_r.at[b - 1])
    returned = rbuf[...].reshape(side * rows, 2 * width)
    sums = lax.dot_general(comb[...], returned, (((0,), (0,)), ((), ())), preferred_element_type=F32)
    part[...] = sums.astype(BF16).reshape(side, tn, 2 * width)
    for d in range(1, side):
        send(part.at[ring(a1 + d, side)], prec.at[d - 1], sum_s.at[d - 1], sum_r.at[d - 1], first_peer(d))
    acc[...] = part[a1].astype(F32)
    mine_rows = pl.ds(pl.multiple_of(c * th, 8), th)
    acc[mine_rows, :] = acc[mine_rows, :] + shared_out
    total = acc[...]
    for d in range(1, side):
        arrived(prec.at[d - 1], sum_s.at[d - 1], sum_r.at[d - 1])
        total = total + prec[d - 1].astype(F32)
    low, high = total[:, :width], total[:, width:]
    first = c == 0
    fsend[...] = jnp.where(first, high, low)
    send(fsend, frecv, part_s.at[5], part_r.at[5], partner)
    keep = jnp.where(first, low, high)
    arrived(frecv, part_s.at[5], part_r.at[5])
    out_ref[...] = (keep + frecv[...]).astype(BF16)
    for copy in pending:
        copy.wait_send()


def build(mesh, most):
    nodes, locals_ = mesh.shape["node"], mesh.shape["local"]
    side, nx = math.isqrt(nodes), locals_ // 2

    def shards(tokens, expert_ids, route_weight, pool_offset, gate_up, down_proj, shared_gate_up, shared_down):
        tn, width = tokens.shape
        experts = pool_offset.shape[1]
        pools = nodes // experts
        half = most // pools // 2
        rows = half * side + 8
        per = min(BLOCKS_PER_CHUNK, side)
        chunks = side // per
        two = shared_gate_up.shape[1]
        ff = two // 2
        cols = two // nx
        crows = per * rows
        hmaj, hmin = nx // 2, nx - 1 - nx // 2
        cfg = dict(
            side=side, nx=nx, experts=experts, pools=pools, half=half, rows=rows, per=per, apart=TICKS_APART
        )
        long_way = side // 2
        dma = pltpu.SemaphoreType.DMA
        scratch = [
            pltpu.VMEM((2 * width, two), BF16),
            pltpu.VMEM((2 * width, two), BF16),
            pltpu.VMEM((2, ff, width), BF16),
            pltpu.VMEM((2, ff, width), BF16),
            pltpu.VMEM((2, tn, width), BF16),
            pltpu.VMEM((side, tn, 2 * width), BF16),
            pltpu.VMEM((side, 2 * experts, tn), F32),
            pltpu.VMEM((experts, side * tn), F32),
            pltpu.VMEM((experts, side * tn), F32),
            pltpu.VMEM((side, rows, 2 * width), BF16),
            pltpu.VMEM((side, rows, 2 * width), BF16),
            pltpu.VMEM((nx, side * 8, cols), F32),
            pltpu.VMEM((chunks, nx, crows, cols), BF16),
            pltpu.VMEM((chunks, hmaj, crows, cols), BF16),
            pltpu.VMEM((chunks, max(hmin, 1), crows, cols), BF16),
            pltpu.VMEM((chunks, nx, crows, cols // 2), BF16),
            pltpu.VMEM((tn // 2, ff), F32),
            pltpu.VMEM((side, rows, 2 * width), BF16),
            pltpu.VMEM((side, rows, 2 * width), BF16),
            pltpu.VMEM((side * rows, side * tn), BF16),
            pltpu.VMEM((side, tn, 2 * width), BF16),
            pltpu.VMEM((side - 1, tn, 2 * width), BF16),
            pltpu.VMEM((tn, 2 * width), F32),
            pltpu.VMEM((tn, width), F32),
            pltpu.VMEM((tn, width), F32),
            dma((6,)), dma((6,)), dma((4,)),
            dma((4 * long_way,)), dma((4 * long_way,)),
            dma((side - 1,)), dma((side - 1,)),
            dma((side - 1,)), dma((side - 1,)),
            dma((chunks * hmaj,)), dma((chunks * hmaj,)),
            dma((chunks * max(hmin, 1),)), dma((chunks * max(hmin, 1),)),
            dma((chunks * hmaj,)), dma((chunks * hmaj,)),
            dma((chunks * max(hmin, 1),)), dma((chunks * max(hmin, 1),)),
            dma((side - 1,)), dma((side - 1,)),
            dma((side - 1,)), dma((side - 1,)),
        ]
        vmem, hbm = pl.BlockSpec(memory_space=pltpu.VMEM), pl.BlockSpec(memory_space=pl.ANY)
        return pl.pallas_call(
            functools.partial(kernel, cfg),
            out_shape=jax.ShapeDtypeStruct((tn, width), BF16),
            in_specs=[vmem] * 4 + [hbm] * 4,
            out_specs=vmem,
            scratch_shapes=scratch,
            compiler_params=pltpu.CompilerParams(
                collective_id=0, has_side_effects=True, vmem_limit_bytes=56 * 1024 * 1024
            ),
        )(
            expert_ids.T, route_weight.T, pool_offset.reshape(experts, 1), tokens,
            gate_up[0], down_proj[0], shared_gate_up, shared_down,
        )

    placed = (
        P("node", "local"),
        P("node", None),
        P("node", None),
        P("node", None),
        P("node", "local", None),
        P("node", None, "local"),
        P("local", None),
        P(None, "local"),
    )
    return jax.shard_map(
        shards, mesh=mesh, in_specs=placed, out_specs=P("node", "local"), check_vma=False
    )


def solution(mesh):
    return build(mesh, MOST)
```

time: 324 us -> 166 us (0.51)
  Pallas kernels: 0 us -> 159 us
  waiting for transfers between devices: 112 us -> 0 us
  blocking collectives: 109 us -> 0 us
  starting transfers between devices: 28.3 us -> 0 us
  local copies, waits for them, and re-layouts: 34.4 us -> 6.52 us
  matrix products: 17.5 us -> 0 us
  between operations: 14.2 us -> 0.01 us
  other arithmetic: 7.74 us -> 0 us
    pallas_call x0 -> x1, Pallas kernels: none -> 159 us  [shards(): pl.pallas_call(functools.partial(kernel, cfg), out_shape=jax.ShapeDtypeSt...]
    reduce_scatter x1 -> x0, waiting for transfers between devices: 66.4 us -> none  [shards(): lax.psum_scatter(expert_term.astype(jnp.bfloat16), 'local', scatter_dimen...]
    all_to_all x1 -> x0, blocking collectives: 62.8 us -> none  [shards(): lax.all_to_all(outgoing, 'node', split_axis=0, concat_axis=0, tiled=True)]
    all_gather x1 -> x0, waiting for transfers between devices: 45.7 us -> none  [shards(): lax.all_gather(hidden, 'local', axis=1, tiled=True)]
    unnamed x1 -> x0, blocking collectives: 28.7 us -> none
    dot_general x6 -> x0, matrix products: 17.5 us -> none  [the longest x2 6.95 us: expert_terms(): lax.dot_general(weights, rows, (((0,), (1,)), ((), ())), preferred_elemen...]
    all_gather x1 -> x0, blocking collectives: 17 us -> none  [shards(): lax.all_gather(shared_hidden, 'local', axis=1, tiled=True)]
    all_to_all x1 -> x0, starting transfers between devices: 14.1 us -> none  [shards(): lax.all_to_all(expert_out.reshape(node_count, capacity, width_local), 'no...]
  transfers between devices with their start and end apart: 7 -> 0, of which waited for: 2 -> 0; matrix products, arithmetic and copies ran while one was open for 16% -> 0% of each run, Pallas kernels for 0% -> 0%
where the time goes in v1:
time: 166 us; the launch traced here: 165 us
  Pallas kernels  159 us (96%)
  local copies, waits for them, and re-layouts  6.52 us (4%)
    pallas_call x1, Pallas kernels, shards(): pl.pallas_call(functools.partial(kernel, cfg), out_shape=jax.ShapeDtypeSt...  159 us
    unnamed x5, local copies, waits for them, and re-layouts  5.11 us

profile of v1, /device:TPU:1, one launch (start us, length us, event | category | flops | bytes accessed | tf_op | source)
XLA Modules:
  0.0 165.3 jit_solution(10497146977157365594)
XLA Ops:
  0.0 0.0 copy-start
  0.0 1.4 copy.10.off_ref
  1.4 2.3 %copy.9 = bf16[1,1024,448]{2,1,0:T(8,128)(2,1)} copy(bf16[1,1024,448]{1,2,0:T(8,128)(2,1)} %param.13) | data formatting | bytes 1835008 | tf_op args[5]
  3.7 0.0 copy-done
  3.7 1.3 copy.11.sdn_hbm
  5.0 158.8 %shard_map.82 = bf16[96,448]{1,0:T(8,128)(2,1)} custom-call(s32[8,96]{1,0:T(8,128)} %bitcast.7, f32[8,96]{1,0:T(8,128)} %bitcast.8, s32[16,1]{1,0:T(8,128)} %copy.10.off_ref, bf16[96,448]{1,0:T(8,128)(2,1)} %tok_ref.1, bf16[448,2048]{1,0:T(8,128)(2,1)} %bitcast.6, bf16[1024,448]{1,0:T(8,128)(2,1)} %bitcast.5, bf16[448,2048]{1,0:T(8,128)(2,1)} %sgu_hbm.1, ...), custom_call_target="tpu_custom_call" | custom-call | tf_op jit(solution)/shard_map/pallas_call | solution.py:410
  163.8 1.5 copy.13
Async XLA Ops:
  0.0 3.7 %copy-start = (bf16[1024,448]{0,1:T(8,128)(2,1)S(1)}, bf16[1024,448]{0,1:T(8,128)(2,1)}, u32[]{:S(2)}) copy-start(bf16[1024,448]{0,1:T(8,128)(2,1)} %param.15) | copy-start | bytes 2752516

commit v2 on v1

v2 whole, which is shorter than its diff:
```python
import functools
import math

import jax
import jax.numpy as jnp
from jax import lax
from jax.experimental import pallas as pl
from jax.experimental.pallas import tpu as pltpu
from jax.sharding import PartitionSpec as P

MESH = pl.DeviceIdType.MESH
MOST = 72
PIECES = 3
CHUNKS = {8: (1, 2, 2, 3), 4: (1, 2, 1), 2: (1, 1)}
STARTS = (0, 0, 1, 2)
DIRECT_SUM = (0, 0, 0, 0)
DIRECT_GATHER = (0, 0, 0, 0)
GROUPS = {8: (3, 1), 4: (2, 1), 2: (1, 1)}
FORWARD_LAG = 2
ADD_LAG = 3
F32 = jnp.float32
BF16 = jnp.bfloat16


def dot(a, b):
    return jnp.dot(a, b, preferred_element_type=F32)


def forward_rows(size, half):
    return -(-size * half // 16) * 16


def groups_of(side):
    groups, chunk, block = [], 0, 0
    for count in GROUPS[side]:
        size = sum(CHUNKS[side][chunk : chunk + count])
        groups.append((chunk, chunk + count - 1, block, size))
        chunk, block = chunk + count, block + size
    return groups


def dot_rows(a, b):
    return lax.dot_general(a, b, (((1,), (1,)), ((), ())), preferred_element_type=F32)


def kernel(
    cfg,
    ids_ref, wt_ref, off_ref, tok_ref, gu_hbm, dn_hbm, sgu_hbm, sdn_hbm,
    out_ref,
    gu, sgu, dn, sdn, tok2, toks, meta, gates, codes, chosen, xs, xsend, ps, pbuf, rmaj, rmin, rdir, hid, hs, obuf, rbuf,
    fwd, frow, comb, acc, fsend, frecv,
    part_s, part_r, loc_sem, tok_s, tok_r, meta_s, meta_r, disp_s, disp_r,
    maj_s, maj_r, min_s, min_r, dir_s, dir_r, gmaj_s, gmaj_r, gmin_s, gmin_r, gdir_s, gdir_r, ret_s, ret_r, fwd_s, fwd_r,
):
    side, nx, experts, pools, half, rows = (cfg[k] for k in ("side", "nx", "experts", "pools", "half", "rows"))
    sizes = CHUNKS[side]
    chunks = len(sizes)
    first_block = [sum(sizes[:k]) for k in range(chunks)]
    groups = groups_of(side)
    lengths = [forward_rows(group[3], half) for group in groups]
    first_row = [sum(lengths[:g]) for g in range(len(groups))]
    tn = tok_ref.shape[0]
    width = tok_ref.shape[1]
    th = tn // 2
    unit_cols = pbuf.shape[2]
    kept = half * side
    shift_pool, shift_side = pools.bit_length() - 1, side.bit_length() - 1

    n, l = lax.axis_index("node"), lax.axis_index("local")
    x, c = lax.div(l, 2), lax.rem(l, 2)
    z, y = lax.div(n, side), lax.rem(n, side)
    a1 = y * (1 - c) + z * c
    a2 = z * (1 - c) + y * c
    stride1 = 1 + (side - 1) * c
    stride2 = side - (side - 1) * c
    sgn = 1 - 2 * c

    def ring(i, count):
        return lax.rem(i + 2 * count, count)

    def node_at(i1, i2):
        return i1 * stride1 + i2 * stride2

    partner = (n, x * 2 + 1 - c)

    def x_peer(step):
        return (n, ring(x + step, nx) * 2 + c)

    def first_peer(step):
        return (node_at(ring(a1 + step, side), a2), l)

    def second_peer(step):
        return (node_at(a1, ring(a2 + step, side)), l)

    offsets = [0]
    for d in range(1, side // 2 + 1):
        offsets += [d, -d]
    offsets = offsets[:side]
    pending = []

    def send(src, dst, s, r, to):
        copy = pltpu.make_async_remote_copy(
            src_ref=src, dst_ref=dst, send_sem=s, recv_sem=r, device_id=to, device_id_type=MESH
        )
        copy.start()
        pending.append(copy)

    def arrived(dst, s, r):
        pltpu.make_async_remote_copy(
            src_ref=dst, dst_ref=dst, send_sem=s, recv_sem=r, device_id=partner, device_id_type=MESH
        ).wait_recv()

    barrier = pltpu.get_barrier_semaphore()
    greeted = [partner] + [x_peer(d) for d in range(1, nx)]
    greeted += [first_peer(d) for d in range(1, side)] + [second_peer(d) for d in range(1, side)]
    for to in greeted:
        pl.semaphore_signal(barrier, inc=1, device_id=to, device_id_type=MESH)

    gu_rows = pl.ds(pl.multiple_of(c * width, 16), width)
    own = [
        pltpu.make_async_copy(sgu_hbm, sgu.at[gu_rows], loc_sem.at[0]),
        pltpu.make_async_copy(gu_hbm, gu.at[gu_rows], loc_sem.at[1]),
        pltpu.make_async_copy(dn_hbm, dn.at[gu_rows], loc_sem.at[2]),
        pltpu.make_async_copy(sdn_hbm, sdn.at[gu_rows], loc_sem.at[3]),
    ]
    for copy in own:
        copy.start()

    ids, wt = ids_ref[...], wt_ref[...]
    expert = lax.broadcasted_iota(jnp.int32, (experts, tn), 0)
    named = jnp.zeros((experts, tn), F32)
    gate_weight = jnp.zeros((experts, tn), F32)
    for k in range(ids.shape[0]):
        hit = ids[k : k + 1, :] == expert
        named = named + jnp.where(hit, 1.0, 0.0)
        gate_weight = gate_weight + jnp.where(hit, wt[k : k + 1, :], 0.0)
    earlier = jnp.where(
        lax.broadcasted_iota(jnp.int32, (tn, tn), 0) < lax.broadcasted_iota(jnp.int32, (tn, tn), 1), 1.0, 0.0
    ).astype(BF16)
    rank = dot(named.astype(BF16), earlier).astype(jnp.int32)
    diagonal = lax.broadcasted_iota(jnp.int32, (experts, experts), 0) == lax.broadcasted_iota(
        jnp.int32, (experts, experts), 1
    )
    offset = jnp.sum(jnp.where(diagonal, off_ref[...], 0), axis=1, keepdims=True)
    code = ((rank + offset) & (pools - 1)) * 32 + (rank >> shift_pool)
    code = jnp.where(named > 0.0, code.astype(F32), -1.0)
    meta[a1] = code
    gates[...] = gate_weight
    tok2[c] = tok_ref[...]

    pl.semaphore_wait(barrier, len(greeted))

    send(tok_ref, tok2.at[c], part_s.at[0], part_r.at[0], partner)

    other_rows = pl.ds(pl.multiple_of((1 - c) * width, 16), width)
    arrived(tok2.at[1 - c], part_s.at[0], part_r.at[0])
    toks[a1] = jnp.concatenate([tok2[0], tok2[1]], axis=1)

    long_way, short_way = side // 2, side - 1 - side // 2

    cut = tn // PIECES

    def token_hop(h, direction, piece):
        hops = long_way if (direction > 0) == (piece % 2 == 0) else short_way
        if h > hops:
            return
        index = ring(a1 - direction * (h - 1), side)
        slot = ((h - 1) * PIECES + piece) * 2 + (direction > 0)
        view = toks.at[index, pl.ds(piece * cut, cut)]
        send(view, view, tok_s.at[slot], tok_r.at[slot], first_peer(direction))

    def token_wait(h, direction, piece):
        hops = long_way if (direction > 0) == (piece % 2 == 0) else short_way
        if h > hops:
            return
        index = ring(a1 - direction * h, side)
        slot = ((h - 1) * PIECES + piece) * 2 + (direction > 0)
        arrived(toks.at[index, pl.ds(piece * cut, cut)], tok_s.at[slot], tok_r.at[slot])

    ways = [(way, piece) for piece in range(PIECES) for way in (1, -1)]
    for h in range(1, long_way + 1):
        for direction, piece in ways:
            if h > 1:
                token_wait(h - 1, direction, piece)
            token_hop(h, direction, piece)
        if h == 1:
            for d in range(1, side):
                send(meta.at[a1], meta.at[a1], meta_s.at[d - 1], meta_r.at[d - 1], first_peer(d))
        if h == max(1, long_way - 2):
            send(gu_hbm, gu.at[gu_rows], part_s.at[2], part_r.at[2], partner)

    for d in range(1, side):
        arrived(meta.at[ring(a1 - d, side)], meta_s.at[d - 1], meta_r.at[d - 1])
    codes[...] = jnp.concatenate([meta[i] + 128.0 * i for i in range(side)], axis=1)
    row = lax.broadcasted_iota(jnp.int32, (rows, 1), 0)
    for b in range(side):
        m = node_at(a1, ring(a2 + offsets[b], side))
        p, e = lax.div(m, experts), lax.rem(m, experts)
        want = (row & (side - 1)) * 128 + (row >> shift_side) + (p * 32 + half * c)
        want = jnp.where(row < kept, want, -5).astype(F32)
        chosen[b * rows : (b + 1) * rows, :] = jnp.where(codes[pl.ds(e, 1), :] == want, 1.0, 0.0).astype(BF16)

    for direction, piece in ways:
        token_wait(long_way, direction, piece)

    def rows_of(k):
        return slice(first_block[k] * rows, (first_block[k] + sizes[k]) * rows)

    def span(k):
        return pl.ds(first_block[k] * rows, sizes[k] * rows)

    def one(b):
        return pl.ds(b * rows, rows)

    near = min(3, side)
    for low, high in ((1, near), (near, side), (0, 1)):
        if low == high:
            continue
        picked = dot(chosen[low * rows : high * rows, :], toks[...].reshape(side * tn, 2 * width)).astype(BF16)
        for b in range(low, high):
            block = picked[(b - low) * rows : (b - low + 1) * rows]
            if b == 0:
                xs[0:rows, :] = block
            else:
                xsend[b * rows : (b + 1) * rows, :] = block
                send(xsend.at[one(b)], xs.at[one(b)], disp_s.at[b - 1], disp_r.at[b - 1], second_peer(offsets[b]))

    def shared_start():
        own[0].wait()
        arrived(sgu.at[other_rows], part_s.at[1], part_r.at[1])
        mine = toks[a1, pl.ds(pl.multiple_of(c * th, 16), th), :]

        def shared_step(q, carry):
            cols = pl.ds(pl.multiple_of(q * unit_cols, 128), unit_cols)
            ps[q] = dot(mine, sgu[:, cols])
            return carry

        lax.fori_loop(0, nx, shared_step, 0)

    own[1].wait()
    arrived(gu.at[other_rows], part_s.at[2], part_r.at[2])
    send(sgu_hbm, sgu.at[gu_rows], part_s.at[1], part_r.at[1], partner)

    hmaj, hmin = nx // 2, nx - 1 - nx // 2
    first_shared = side - th // 8
    first_shared_chunk = [k for k in range(chunks) if first_block[k] + sizes[k] > first_shared][0]

    def to_x(off):
        return ring(x + sgn * off, nx)

    def start_chunk(k):
        for i in range(sizes[k]):
            b = first_block[k] + i
            if b > 0:
                arrived(xs.at[one(b)], disp_s.at[b - 1], disp_r.at[b - 1])
        if k == first_shared_chunk:
            shared_start()
        rows_in = xs[rows_of(k), :]

        def step(i, carry):
            q = to_x(hmaj - i)
            cols = pl.ds(pl.multiple_of(q * unit_cols, 128), unit_cols)
            value = dot(rows_in, gu[:, cols])
            pieces = []
            for j in range(sizes[k]):
                number = first_block[k] + j - first_shared
                shared = value[j * rows + kept : (j + 1) * rows]
                if number >= 0:
                    shared = ps[q, number * 8 : (number + 1) * 8, :]
                pieces += [value[j * rows : j * rows + kept], shared]
            pbuf[q, rows_of(k), :] = jnp.concatenate(pieces, axis=0).astype(BF16)
            return carry

        lax.fori_loop(0, nx, step, 0)
        if k == 0:
            send(dn_hbm, dn.at[gu_rows], part_s.at[3], part_r.at[3], partner)
            send(sdn_hbm, sdn.at[gu_rows], part_s.at[4], part_r.at[4], partner)
        if DIRECT_SUM[k]:
            for d in range(1, nx):
                slot = k * (nx - 1) + d - 1
                send(pbuf.at[ring(x + d, nx), span(k)], rdir.at[d - 1, span(k)], dir_s.at[slot], dir_r.at[slot], x_peer(d))
        else:
            sum_send(k, 0, hmaj, 1, rmaj, maj_s, maj_r)
            sum_send(k, 0, hmin, -1, rmin, min_s, min_r)

    def sum_send(k, h, hops, way, recv, s, r):
        if h < hops:
            slot = k * hops + h
            view = pbuf.at[to_x(way * (hops - h)), span(k)]
            send(view, recv.at[h, span(k)], s.at[slot], r.at[slot], x_peer(sgn * way))

    def sum_hop(k, h, hops, way, recv, s, r):
        if h < hops:
            slot = k * hops + h
            arrived(recv.at[h - 1, span(k)], s.at[slot - 1], r.at[slot - 1])
            q = to_x(way * (hops - h))
            value = pbuf[q, rows_of(k), :].astype(F32) + recv[h - 1, rows_of(k), :].astype(F32)
            pbuf[q, rows_of(k), :] = value.astype(BF16)
            sum_send(k, h, hops, way, recv, s, r)

    def sum_hops(k, h):
        sum_hop(k, h, hmaj, 1, rmaj, maj_s, maj_r)
        sum_hop(k, h, hmin, -1, rmin, min_s, min_r)

    def activate(k):
        total = pbuf[x, rows_of(k), :].astype(F32)
        if DIRECT_SUM[k]:
            for d in range(1, nx):
                slot = k * (nx - 1) + d - 1
                arrived(rdir.at[d - 1, span(k)], dir_s.at[slot], dir_r.at[slot])
                total = total + rdir[d - 1, rows_of(k), :].astype(F32)
        else:
            for hops, recv, s, r in ((hmaj, rmaj, maj_s, maj_r), (hmin, rmin, min_s, min_r)):
                if hops:
                    slot = k * hops + hops - 1
                    arrived(recv.at[hops - 1, span(k)], s.at[slot], r.at[slot])
                    total = total + recv[hops - 1, rows_of(k), :].astype(F32)
        wide = unit_cols // 2
        left, right = total[:, :wide], total[:, wide:]
        low = lax.broadcasted_iota(jnp.int32, left.shape, 1) < wide // 2
        gate = jnp.where(low, left, pltpu.roll(right, wide // 2, 1))
        upper = jnp.where(low, pltpu.roll(left, wide // 2, 1), right)
        hid[x, rows_of(k), :] = (gate / (1.0 + jnp.exp(-gate)) * upper).astype(BF16)
        if DIRECT_GATHER[k]:
            view = hid.at[x, span(k)]
            for d in range(1, nx):
                slot = k * (nx - 1) + d - 1
                send(view, view, gdir_s.at[slot], gdir_r.at[slot], x_peer(d))
        else:
            gather_hop(k, 1, hmaj, 1, gmaj_s, gmaj_r)
            gather_hop(k, 1, hmin, -1, gmin_s, gmin_r)

    def gather_hop(k, h, hops, way, s, r):
        if h <= hops:
            view = hid.at[to_x(-way * (h - 1)), span(k)]
            slot = k * hops + h - 1
            send(view, view, s.at[slot], r.at[slot], x_peer(sgn * way))

    def gather_wait(k, h, hops, way, s, r):
        if h <= hops:
            slot = k * hops + h - 1
            arrived(hid.at[to_x(-way * h), span(k)], s.at[slot], r.at[slot])

    def gather_hops(k, h):
        gather_wait(k, h, hmaj, 1, gmaj_s, gmaj_r)
        gather_hop(k, h + 1, hmaj, 1, gmaj_s, gmaj_r)
        gather_wait(k, h, hmin, -1, gmin_s, gmin_r)
        gather_hop(k, h + 1, hmin, -1, gmin_s, gmin_r)

    def finish_chunk(k):
        if DIRECT_GATHER[k]:
            for d in range(1, nx):
                slot = k * (nx - 1) + d - 1
                arrived(hid.at[ring(x - d, nx), span(k)], gdir_s.at[slot], gdir_r.at[slot])
        else:
            gather_hops(k, hmaj)
        if k == 0:
            own[2].wait()
            arrived(dn.at[other_rows], part_s.at[3], part_r.at[3])
        hidden = jnp.concatenate([hid[q, rows_of(k), :] for q in range(nx)], axis=1)
        result = dot_rows(hidden, dn[...]).astype(BF16)
        for i in range(sizes[k]):
            b = first_block[k] + i
            block = result[i * rows : (i + 1) * rows]
            if b == 0:
                rbuf[0:rows, :] = block
            else:
                obuf[b * rows : (b + 1) * rows, :] = block
                send(obuf.at[one(b)], rbuf.at[one(b)], ret_s.at[b - 1], ret_r.at[b - 1], second_peer(-offsets[b]))
        for i in range(sizes[k]):
            number = first_block[k] + i - first_shared
            if number >= 0:
                top = (i + 1) * rows - 16
                hs[number * 8 : (number + 1) * 8, :] = hidden[top : top + 16].astype(F32)[8:16]

    def place(g, index):
        node_index, which = jnp.zeros_like(index), jnp.zeros_like(index)
        for i in range(1, side):
            node_index = node_index + jnp.where(index >= i * lengths[g], 1, 0)
        number = index - node_index * lengths[g]
        for i in range(1, groups[g][3]):
            which = which + jnp.where(number >= i * half, 1, 0)
        return node_index, number < groups[g][3] * half, which, number - which * half

    def forward_span(g):
        return pl.ds(first_row[g], lengths[g])

    def forward_group(g):
        _, _, block, size = groups[g]
        for b in range(block, block + size):
            if b > 0:
                arrived(rbuf.at[one(b)], ret_s.at[b - 1], ret_r.at[b - 1])
        length = lengths[g]
        shape = (side * length, size * rows)
        node_index, used, which, slot = place(g, lax.broadcasted_iota(jnp.int32, (shape[0], 1), 0))
        source = jnp.where(used, which * rows + slot * side + node_index, -1)
        moved = jnp.where(lax.broadcasted_iota(jnp.int32, shape, 1) == source, 1.0, 0.0).astype(BF16)
        result = dot(moved, rbuf[block * rows : (block + size) * rows, :]).astype(BF16)
        for i in range(side):
            fwd[i, first_row[g] : first_row[g] + length, :] = result[i * length : (i + 1) * length]
        for d in range(1, side):
            slot = g * (side - 1) + d - 1
            send(
                fwd.at[ring(a1 + d, side), forward_span(g)], frow.at[a1, forward_span(g)],
                fwd_s.at[slot], fwd_r.at[slot], first_peer(d),
            )
        frow[a1, first_row[g] : first_row[g] + length, :] = fwd[a1, first_row[g] : first_row[g] + length, :]

    def weigh_group(g):
        _, _, block, size = groups[g]
        length = lengths[g]
        node_index, used, which, slot = place(g, lax.broadcasted_iota(jnp.int32, (1, side * length), 1))
        shift = jnp.zeros_like(which)
        for i in range(size):
            shift = jnp.where(which == i, offsets[block + i], shift)
        second = (a2 + shift + side) & (side - 1)
        m = node_index * stride1 + second * stride2
        want = (m >> (experts.bit_length() - 1)) * 32 + slot + half * c
        want = jnp.where(used, want, -5).astype(F32)
        chosen_expert = lax.broadcasted_iota(jnp.int32, (experts, side * length), 0) == (m & (experts - 1))
        chosen_expert = jnp.where(chosen_expert, 1.0, 0.0).astype(BF16)
        ends = (((0,), (0,)), ((), ()))
        found = lax.dot_general(meta[a1].astype(BF16), chosen_expert, ends, preferred_element_type=F32)
        weight = lax.dot_general(gates[...].astype(BF16), chosen_expert, ends, preferred_element_type=F32)
        comb[:, first_row[g] * side : (first_row[g] + length) * side] = jnp.where(found == want, weight, 0.0).astype(BF16)

    def add_group(g):
        length = lengths[g]
        for d in range(1, side):
            slot = g * (side - 1) + d - 1
            arrived(frow.at[ring(a1 - d, side), forward_span(g)], fwd_s.at[slot], fwd_r.at[slot])
        landed = frow[:, first_row[g] : first_row[g] + length, :].reshape(side * length, 2 * width)
        acc[...] += dot(comb[:, first_row[g] * side : (first_row[g] + length) * side], landed)

    def shared_finish():
        own[3].wait()
        arrived(sdn.at[other_rows], part_s.at[4], part_r.at[4])
        mine_rows = pl.ds(pl.multiple_of(c * th, 8), th)
        acc[mine_rows, :] += dot_rows(hs[...].astype(BF16), sdn[...])

    schedule = []
    for k in range(chunks):
        steps = [start_chunk]
        if not DIRECT_SUM[k]:
            steps += [functools.partial(lambda h, k: sum_hops(k, h), h) for h in range(1, hmaj)]
        steps += [activate]
        if not DIRECT_GATHER[k]:
            steps += [functools.partial(lambda h, k: gather_hops(k, h), h) for h in range(1, hmaj)]
        steps += [finish_chunk]
        for i, f in enumerate(steps):
            schedule.append((STARTS[k] + i, k, f))
        finish = STARTS[k] + len(steps) - 1
        for g, group in enumerate(groups):
            if group[1] == k:
                schedule.append((STARTS[0] + 2 + g, chunks, functools.partial(lambda g, _: weigh_group(g), g)))
                schedule.append((finish + FORWARD_LAG, k, functools.partial(lambda g, _: forward_group(g), g)))
                schedule.append((finish + ADD_LAG, k, functools.partial(lambda g, _: add_group(g), g)))
    schedule.sort(key=lambda item: item[:2])
    acc[...] = jnp.zeros_like(acc)
    for _, k, f in schedule:
        f(k)
        if f is finish_chunk and k == chunks - 1:
            shared_finish()
    total = acc[...]
    low, high = total[:, :width], total[:, width:]
    first = c == 0
    fsend[...] = jnp.where(first, high, low)
    send(fsend, frecv, part_s.at[5], part_r.at[5], partner)
    keep = jnp.where(first, low, high)
    arrived(frecv, part_s.at[5], part_r.at[5])
    out_ref[...] = (keep + frecv[...]).astype(BF16)
    for copy in pending:
        copy.wait_send()


def build(mesh, most):
    nodes, locals_ = mesh.shape["node"], mesh.shape["local"]
    side, nx = math.isqrt(nodes), locals_ // 2

    def shards(tokens, expert_ids, route_weight, pool_offset, gate_up, down_proj, shared_gate_up, shared_down):
        tn, width = tokens.shape
        experts = pool_offset.shape[1]
        pools = nodes // experts
        half = most // pools // 2
        rows = half * side + 8
        sizes = CHUNKS[side]
        chunks = len(sizes)
        forwarded = sum(forward_rows(group[3], half) for group in groups_of(side))
        parcels = len(GROUPS[side]) * (side - 1)
        two = shared_gate_up.shape[1]
        ff = two // 2
        cols = two // nx
        every = side * rows
        hmaj, hmin = nx // 2, max(nx - 1 - nx // 2, 1)
        cfg = dict(side=side, nx=nx, experts=experts, pools=pools, half=half, rows=rows)
        long_way = side // 2
        dma = pltpu.SemaphoreType.DMA
        scratch = [
            pltpu.VMEM((2 * width, two), BF16),
            pltpu.VMEM((2 * width, two), BF16),
            pltpu.VMEM((2 * width, ff), BF16),
            pltpu.VMEM((2 * width, ff), BF16),
            pltpu.VMEM((2, tn, width), BF16),
            pltpu.VMEM((side, tn, 2 * width), BF16),
            pltpu.VMEM((side, experts, tn), F32),
            pltpu.VMEM((experts, tn), F32),
            pltpu.VMEM((experts, side * tn), F32),
            pltpu.VMEM((every, side * tn), BF16),
            pltpu.VMEM((every, 2 * width), BF16),
            pltpu.VMEM((every, 2 * width), BF16),
            pltpu.VMEM((nx, tn // 2, cols), F32),
            pltpu.VMEM((nx, every, cols), BF16),
            pltpu.VMEM((hmaj, every, cols), BF16),
            pltpu.VMEM((hmin, every, cols), BF16),
            pltpu.VMEM((nx - 1, every, cols), BF16),
            pltpu.VMEM((nx, every, cols // 2), BF16),
            pltpu.VMEM((tn // 2, ff), F32),
            pltpu.VMEM((every, 2 * width), BF16),
            pltpu.VMEM((every, 2 * width), BF16),
            pltpu.VMEM((side, forwarded, 2 * width), BF16),
            pltpu.VMEM((side, forwarded, 2 * width), BF16),
            pltpu.VMEM((tn, side * forwarded), BF16),
            pltpu.VMEM((tn, 2 * width), F32),
            pltpu.VMEM((tn, width), F32),
            pltpu.VMEM((tn, width), F32),
            dma((6,)), dma((6,)), dma((4,)),
            dma((2 * PIECES * long_way,)), dma((2 * PIECES * long_way,)),
            dma((side - 1,)), dma((side - 1,)),
            dma((side - 1,)), dma((side - 1,)),
            dma((chunks * hmaj,)), dma((chunks * hmaj,)),
            dma((chunks * hmin,)), dma((chunks * hmin,)),
            dma((chunks * (nx - 1),)), dma((chunks * (nx - 1),)),
            dma((chunks * hmaj,)), dma((chunks * hmaj,)),
            dma((chunks * hmin,)), dma((chunks * hmin,)),
            dma((chunks * (nx - 1),)), dma((chunks * (nx - 1),)),
            dma((side - 1,)), dma((side - 1,)),
            dma((parcels,)), dma((parcels,)),
        ]
        vmem, hbm = pl.BlockSpec(memory_space=pltpu.VMEM), pl.BlockSpec(memory_space=pl.ANY)
        return pl.pallas_call(
            functools.partial(kernel, cfg),
            out_shape=jax.ShapeDtypeStruct((tn, width), BF16),
            in_specs=[vmem] * 4 + [hbm] * 4,
            out_specs=vmem,
            scratch_shapes=scratch,
            compiler_params=pltpu.CompilerParams(
                collective_id=0, has_side_effects=True, vmem_limit_bytes=56 * 1024 * 1024
            ),
        )(
            expert_ids.T, route_weight.T, pool_offset, tokens,
            gate_up[0], down_proj[0].T, shared_gate_up, shared_down.T,
        )

    placed = (
        P("node", "local"),
        P("node", None),
        P("node", None),
        P("node", None),
        P("node", "local", None),
        P("node", None, "local"),
        P("local", None),
        P(None, "local"),
    )
    return jax.shard_map(
        shards, mesh=mesh, in_specs=placed, out_specs=P("node", "local"), check_vma=False
    )


def solution(mesh):
    return build(mesh, MOST)
```

time: 166 us -> 132 us (0.80)
  Pallas kernels: 159 us -> 129 us
  local copies, waits for them, and re-layouts: 6.52 us -> 1.54 us
    pallas_call x1, Pallas kernels: 159 us -> 129 us  [shards(): pl.pallas_call(functools.partial(kernel, cfg), out_shape=jax.ShapeDtypeSt...]
    unnamed x5 -> x1, local copies, waits for them, and re-layouts: 5.11 us -> 1.54 us
where the time goes in v2:
time: 132 us; the launch traced here: 130 us
  Pallas kernels  129 us (98%)
  local copies, waits for them, and re-layouts  1.54 us (1%)
    pallas_call x1, Pallas kernels, shards(): pl.pallas_call(functools.partial(kernel, cfg), out_shape=jax.ShapeDtypeSt...  129 us

profile of v2, /device:TPU:1, one launch (start us, length us, event | category | flops | bytes accessed | tf_op | source)
XLA Modules:
  0.0 130.4 jit_solution(16527895087302731212)
XLA Ops:
  0.0 128.9 %shard_map.82 = bf16[96,448]{1,0:T(8,128)(2,1)} custom-call(s32[8,96]{1,0:T(8,128)} %bitcast.10, f32[8,96]{1,0:T(8,128)} %bitcast.11, s32[1,16]{1,0:T(1,128)} %off_ref.1, bf16[96,448]{1,0:T(8,128)(2,1)} %tok_ref.1, bf16[448,2048]{1,0:T(8,128)(2,1)} %bitcast.7, bf16[448,1024]{1,0:T(8,128)(2,1)} %bitcast.8, bf16[448,2048]{1,0:T(8,128)(2,1)} %sgu_hbm.1, ...), custom_call_target="tpu_custom_call" | custom-call | tf_op jit(solution)/shard_map/pallas_call | solution.py:540
  128.9 1.5 %copy.10 = bf16[96,448]{1,0:T(8,128)(2,1)} copy(bf16[96,448]{1,0:T(8,128)(2,1)} %shard_map.82) | data formatting | bytes 172032

commit v3 on v2

--- a/solution.py
+++ b/solution.py
@@ -10,9 +10,10 @@
 
 MESH = pl.DeviceIdType.MESH
 MOST = 72
+OFFSETS = {8: (0, 1, -1, 3, -3, 4, 2, -2), 4: (0, 1, -1, 2), 2: (0, 1)}
 PIECES = 3
-CHUNKS = {8: (1, 2, 2, 3), 4: (1, 2, 1), 2: (1, 1)}
-STARTS = (0, 0, 1, 2)
+CHUNKS = {8: (1, 2, 3, 2), 4: (1, 2, 1), 2: (1, 1)}
+STARTS = (0, 0, 1, 1)
 DIRECT_SUM = (0, 0, 0, 0)
 DIRECT_GATHER = (0, 0, 0, 0)
 GROUPS = {8: (3, 1), 4: (2, 1), 2: (1, 1)}
@@ -92,10 +93,7 @@
     def second_peer(step):
         return (node_at(a1, ring(a2 + step, side)), l)
 
-    offsets = [0]
-    for d in range(1, side // 2 + 1):
-        offsets += [d, -d]
-    offsets = offsets[:side]
+    offsets = OFFSETS[side]
     pending = []
 
     def send(src, dst, s, r, to):

time: 132 us -> 131 us (level)
  no operation moved by 1% of the time
where the time goes in v3:
time: 131 us
  Pallas kernels  129 us (98%)
  local copies, waits for them, and re-layouts  1.54 us (1%)
    pallas_call x1, Pallas kernels, shards(): pl.pallas_call(functools.partial(kernel, cfg), out_shape=jax.ShapeDtypeSt...  129 us

profile of v3, /device:TPU:1, one launch (start us, length us, event | category | flops | bytes accessed | tf_op | source)
XLA Modules:
  0.0 130.7 jit_solution(299773069373668689)
XLA Ops:
  0.0 129.2 %shard_map.82 = bf16[96,448]{1,0:T(8,128)(2,1)} custom-call(s32[8,96]{1,0:T(8,128)} %bitcast.10, f32[8,96]{1,0:T(8,128)} %bitcast.11, s32[1,16]{1,0:T(1,128)} %off_ref.1, bf16[96,448]{1,0:T(8,128)(2,1)} %tok_ref.1, bf16[448,2048]{1,0:T(8,128)(2,1)} %bitcast.7, bf16[448,1024]{1,0:T(8,128)(2,1)} %bitcast.8, bf16[448,2048]{1,0:T(8,128)(2,1)} %sgu_hbm.1, ...), custom_call_target="tpu_custom_call" | custom-call | tf_op jit(solution)/shard_map/pallas_call | solution.py:538
  129.2 1.5 %copy.10 = bf16[96,448]{1,0:T(8,128)(2,1)} copy(bf16[96,448]{1,0:T(8,128)(2,1)} %shard_map.82) | data formatting | bytes 172032
